TPU v7x, 512 devices: a whole 4x8x8 slice. The times are simulated.
512 devices in a mesh: ctx: 32 (over x_hi, z, core), dp: 16 (over y, x_lo).
Axes of the slice: x: 4 (x_hi: 2, x_lo: 2; x = x_hi * 2 + x_lo), y: 8, z: 8, core: 2. Of those that a mesh axis runs over, the one named last changes fastest.
Arguments:
- x_tokens: bfloat16 [16, 4096, 8192], P('dp', 'ctx'), may hold values from -6 to 6
- grad_out: bfloat16 [16, 4096, 8192], P('dp', 'ctx'), may hold values from -0.011962891 to 0.011962891
- step_raw: bfloat16 [16, 4096, 128], P('dp', 'ctx'), may hold values from -5 to 5
- step_bias: float32 [128], P('ctx'), may hold values from -1.5 to 0.5
- decay_log: float32 [128], P('ctx'), may hold values from -20 to -3, as said below
- b_proj: bfloat16 [16, 4096, 512], P('dp', 'ctx'), may hold values from -2.09375 to 2.09375
- c_proj: bfloat16 [16, 4096, 512], P('dp', 'ctx'), may hold values from -2.09375 to 2.09375
Outputs:
- grad_b: float32 [16, 4096, 512], P('dp', 'ctx')
- grad_c: float32 [16, 4096, 512], P('dp', 'ctx')
- grad_step: bfloat16 [16, 4096, 128], P('dp', 'ctx')
- grad_decay: float32 [128], P('ctx')
- grad_bias: float32 [128], P('ctx')
- grad_skip: float32 [128], P('ctx')
Inputs may be any that keep to these rules, and one draw needn't show every extreme that they name: Every head's decay rate exp(decay_log) is positive and below 1 / 20.
All inputs are finite; a program needn't handle non-finite values.
Results may differ from a plain program's by a relative error of at most 0.015.
Values may be sent and summed in bfloat16 or wider, within the bound.
A program may use at most 128 MiB of HBM per device.

v0:
```python
from functools import partial

import jax
import jax.numpy as jnp
from jax import lax
from jax.sharding import PartitionSpec as P

HEADDIM = 64
STATE = 128
BLOCK = 256


def product(form, left, right):
    return jnp.einsum(form, left, right, preferred_element_type=jnp.float32)


def block_step(state_in, block_items, decay_rate):
    x_block, step_block, b_block, c_block = block_items
    width = step_block.shape[0]
    b_half = b_block.astype(jnp.bfloat16)
    c_half = c_block.astype(jnp.bfloat16)
    cum_decay = jnp.cumsum(step_block * decay_rate[None, :], axis=0)
    scores = jnp.dot(c_half, b_half.T, preferred_element_type=jnp.float32)
    positions = jnp.arange(width, dtype=jnp.int32)
    causal = positions[:, None] >= positions[None, :]
    gap_sum = jnp.where(causal[:, :, None], cum_decay[:, None, :] - cum_decay[None, :, :], -jnp.inf)
    mixing = (scores[:, :, None] * jnp.exp(gap_sum) * step_block[None, :, :]).astype(jnp.bfloat16)
    inner_part = product("ijh,jhp->ihp", mixing, x_block)
    carried = (
        jnp.einsum("in,hnp->ihp", c_block, state_in, precision=lax.Precision.HIGHEST)
        * jnp.exp(cum_decay)[:, :, None]
    )
    tail_sum = cum_decay[-1]
    feed_rows = (
        b_block[:, None, :] * (jnp.exp(tail_sum[None, :] - cum_decay) * step_block)[:, :, None]
    ).astype(jnp.bfloat16)
    fresh_state = product("jhn,jhp->hnp", feed_rows, x_block)
    state_out = jnp.exp(tail_sum)[:, None, None] * state_in + fresh_state
    return (state_out, inner_part + carried)


def local_grads(x_heads, grad_heads, raw_heads, b_rows, c_rows, step_bias, decay_log, block):
    seq_len, head_count = raw_heads.shape
    blocks = seq_len // block

    def objective(raw_value, bias_value, log_value, b_value, c_value):
        step_size = jax.nn.softplus(raw_value + bias_value[None, :])
        decay_rate = -jnp.exp(log_value)
        stepper = jax.checkpoint(partial(block_step, decay_rate=decay_rate))
        start = jnp.zeros((head_count, STATE, HEADDIM), jnp.float32)
        _, outputs = lax.scan(
            stepper,
            start,
            (
                x_heads.reshape(blocks, block, head_count, HEADDIM),
                step_size.reshape(blocks, block, head_count),
                b_value.reshape(blocks, block, STATE),
                c_value.reshape(blocks, block, STATE),
            ),
        )
        return jnp.sum(
            outputs * grad_heads.reshape(blocks, block, head_count, HEADDIM).astype(jnp.float32)
        )

    gradients = jax.grad(objective, argnums=(0, 1, 2, 3, 4))(
        raw_heads.astype(jnp.float32),
        step_bias,
        decay_log,
        b_rows.astype(jnp.float32),
        c_rows.astype(jnp.float32),
    )
    grad_raw, grad_bias, grad_decay, grad_brows, grad_crows = gradients
    grad_skip = product("lhp,lhp->h", x_heads, grad_heads)
    return (
        grad_brows.astype(jnp.bfloat16),
        grad_crows.astype(jnp.bfloat16),
        grad_raw.astype(jnp.bfloat16),
        grad_decay,
        grad_bias,
        grad_skip,
    )


def local(x_tokens, grad_out, step_raw, step_bias, decay_log, b_proj, c_proj):
    shards = lax.axis_size("ctx")
    tok_rows = x_tokens.shape[1]
    head_count = step_bias.shape[0]
    groups = b_proj.shape[2] // STATE
    repeat = shards // groups
    seq_len = tok_rows * shards
    x_split = x_tokens.reshape(tok_rows, shards, head_count * HEADDIM)
    grad_split = grad_out.reshape(tok_rows, shards, head_count * HEADDIM)
    raw_split = step_raw.reshape(tok_rows, shards, head_count)
    x_heads, grad_heads, raw_heads = (
        lax.all_to_all(x_split, "ctx", split_axis=1, concat_axis=0, tiled=True),
        lax.all_to_all(grad_split, "ctx", split_axis=1, concat_axis=0, tiled=True),
        lax.all_to_all(raw_split, "ctx", split_axis=1, concat_axis=0, tiled=True),
    )
    b_whole, c_whole = (
        lax.all_gather(b_proj[0], "ctx", axis=0, tiled=True),
        lax.all_gather(c_proj[0], "ctx", axis=0, tiled=True),
    )
    group_index = lax.axis_index("ctx") // repeat
    b_rows = lax.dynamic_slice_in_dim(b_whole, group_index * STATE, STATE, 1)
    c_rows = lax.dynamic_slice_in_dim(c_whole, group_index * STATE, STATE, 1)
    results = local_grads(
        x_heads.reshape(seq_len, head_count, HEADDIM),
        grad_heads.reshape(seq_len, head_count, HEADDIM),
        raw_heads.reshape(seq_len, head_count),
        b_rows,
        c_rows,
        step_bias,
        decay_log,
        BLOCK,
    )
    grad_brows, grad_crows, grad_raw, grad_decay, grad_bias, grad_skip = results
    back_b, back_c, back_step = (
        lax.all_to_all(
            grad_brows.reshape(seq_len, 1, STATE), "ctx", split_axis=0, concat_axis=1, tiled=True
        ),
        lax.all_to_all(
            grad_crows.reshape(seq_len, 1, STATE), "ctx", split_axis=0, concat_axis=1, tiled=True
        ),
        lax.all_to_all(
            grad_raw.reshape(seq_len, 1, head_count), "ctx", split_axis=0, concat_axis=1, tiled=True
        ),
    )
    grad_b = (
        back_b.astype(jnp.float32)
        .reshape(tok_rows, groups, repeat, STATE)
        .sum(axis=2)
        .reshape(1, tok_rows, groups * STATE)
    )
    grad_c = (
        back_c.astype(jnp.float32)
        .reshape(tok_rows, groups, repeat, STATE)
        .sum(axis=2)
        .reshape(1, tok_rows, groups * STATE)
    )
    grad_step = back_step.reshape(1, tok_rows, shards * head_count)
    grad_decay, grad_bias, grad_skip = lax.psum((grad_decay, grad_bias, grad_skip), "dp")
    return (grad_b, grad_c, grad_step, grad_decay, grad_bias, grad_skip)


def solution(mesh):
    return jax.shard_map(
        local,
        mesh=mesh,
        in_specs=(
            P("dp", "ctx", None),
            P("dp", "ctx", None),
            P("dp", "ctx", None),
            P("ctx"),
            P("ctx"),
            P("dp", "ctx", None),
            P("dp", "ctx", None),
        ),
        out_specs=(
            P("dp", "ctx", None),
            P("dp", "ctx", None),
            P("dp", "ctx", None),
            P("ctx"),
            P("ctx"),
            P("ctx"),
        ),
        check_vma=False,
    )
```

profile of v0, /device:TPU:1, one launch (start us, length us, event | category | flops | bytes accessed | tf_op | source)
XLA Modules:
  0.0 812.5 jit_solution(3122604933701743832)
XLA Ops:
  9.4 14.4 %all-to-all-start = ((bf16[128,32,4]{0,2,1:T(4,128)(2,1)}), bf16[128,32,4]{0,2,1:T(4,128)(2,1)S(1)}, u32[]{:S(2)}, u32[]{:S(2)}) async-start(bf16[128,32,4]{0,2,1:T(4,128)(2,1)} %bitcast.2), calls=%async_computation | async-start | bytes 65536 | tf_op jit(solution)/shard_map/all_to_all | solution.py:97
  27.9 5.3 all-to-all-done
  33.2 4.6 all-to-all-start.1
  42.7 51.7 %all-to-all-done.1 = bf16[128,32,256]{0,2,1:T(8,128)(2,1)S(1)} async-done(((bf16[128,32,256]{0,2,1:T(8,128)(2,1)}), bf16[128,32,256]{0,2,1:T(8,128)(2,1)S(1)}, u32[]{:S(2)}, u32[]{:S(2)}) %all-to-all-start.1) | async-done | bytes 2097184 | tf_op jit(solution)/shard_map/all_to_all | solution.py:95
  95.7 5.7 all-to-all-start.2
  114.9 42.9 %all-to-all-done.2 = bf16[128,32,256]{0,2,1:T(8,128)(2,1)S(1)} async-done(((bf16[128,32,256]{0,2,1:T(8,128)(2,1)}), bf16[128,32,256]{0,2,1:T(8,128)(2,1)S(1)}, u32[]{:S(2)}, u32[]{:S(2)}) %all-to-all-start.2) | async-done | bytes 2097184 | tf_op jit(solution)/shard_map/all_to_all | solution.py:96
  162.6 5.2 reshape.383
  167.8 57.2 %all-gather.7.cloned.1.call-done = bf16[1,4096,512]{2,1,0:T(8,128)(2,1)} async-done(((bf16[1,128,512]{2,1,0:T(8,128)(2,1)}), bf16[1,4096,512]{2,1,0:T(8,128)(2,1)}) %all-gather.7.cloned.1.call-update) | async-done | bytes 4194320 | tf_op jit(solution)/shard_map/all_gather | solution.py:101
  229.9 99.5 %while.36 = (s32[]{:T(128)}, f32[4,128,64]{1,2,0:T(8,128)S(1)}, f32[16,4,128,64]{2,3,1,0:T(8,128)}, f32[16,256,4]{1,2,0:T(4,128)}, f32[1,4]{1,0:T(1,128)S(1)}, /...) while((s32[]{:T(128)}, f32[4,128,64]{1,2,0:T(8,128)S(1)}, ...), condition=%wide.region_3.4_spmd.clone, body=%wide.region_0.3_spmd.clone.sunk | while | flops 17304592 | bytes 1106548 | solution.py:51
  332.5 344.9 %while.37 = (s32[]{:T(128)}, f32[4]{0:T(128)S(1)}, f32[4,128,64]{1,2,0:T(8,128)S(1)}, f32[16,256,4]{1,0,2:T(8,128)}, bf16[16,256,128]{2,1,0:T(8,128)(2,1)}, /*in...) while((s32[]{:T(128)}, f32[4]{0:T(128)S(1)}, ...), condition=%wide.region_19.20_spmd.clone, body=%wide.region_4.19_spmd.clone.sunk | while | flops 407912512 | bytes 8078624 | solution.py:51
  344.0 5.0 reduce-window.70
  365.6 5.0 reduce-window.70
  387.1 5.0 reduce-window.70
  408.7 5.0 reduce-window.70
  430.3 5.0 reduce-window.70
  451.8 5.0 reduce-window.70
  473.4 5.0 reduce-window.70
  494.9 5.0 reduce-window.70
  516.5 5.0 reduce-window.70
  538.0 5.0 reduce-window.70
  559.6 5.0 reduce-window.70
  581.1 5.0 reduce-window.70
  602.7 5.0 reduce-window.70
  624.3 5.0 reduce-window.70
  645.8 5.0 reduce-window.70
  667.4 5.0 reduce-window.70
  695.1 5.1 all-to-all-done.5
  700.2 4.7 all-to-all-start.4
  710.4 22.2 %all-to-all-done.4 = bf16[32,2,8192]{2,1,0:T(2,128)(2,1)S(1)} async-done(((bf16[32,2,8192]{2,1,0:T(2,128)(2,1)}), bf16[32,2,8192]{2,1,0:T(2,128)(2,1)S(1)}, u32[]{:S(2)}, u32[]{:S(2)}) %all-to-all-start.4) | async-done | bytes 1048608 | tf_op jit(solution)/shard_map/all_to_all | solution.py:121
  732.6 6.6 all-to-all-start.3
  753.0 28.1 %all-reduce.1 = (f32[4]{0:T(128)}, f32[4]{0:T(128)}, f32[4]{0:T(128)}) all-reduce(f32[4]{0:T(128)S(1)} %negate_multiply_fusion, f32[4]{0:T(128)S(1)} %fusion.44, f32[4]{0:T(128)S(1)} %fusion.40), channel_id=1, replica_groups=mesh['ctx'=32,'dp'=16] {'dp'}, use_global_device_ids=true, to_apply=%region_22.23 | all-reduce | flops 12 | bytes 96 | tf_op jit(solution)/shard_map/psum | solution.py:141
  795.0 5.8 reshape.418
  (1102 shorter events, 455.7 us)
Async XLA Ops:
  7.2 160.7 %all-gather.5.cloned.1.call-start = ((), (), s32[]{:S(2)}) async-start(), calls=%async_computation.6 | async-start | bytes 4325376 | tf_op jit(solution)/shard_map/all_gather | solution.py:100
  9.4 23.9 %all-to-all-start = ((bf16[128,32,4]{0,2,1:T(4,128)(2,1)}), bf16[128,32,4]{0,2,1:T(4,128)(2,1)S(1)}, u32[]{:S(2)}, u32[]{:S(2)}) async-start(bf16[128,32,4]{0,2,1:T(4,128)(2,1)} %bitcast.2), calls=%async_computation | async-start | bytes 65536 | tf_op jit(solution)/shard_map/all_to_all | solution.py:97
  33.2 61.1 %all-to-all-start.1 = ((bf16[128,32,256]{0,2,1:T(8,128)(2,1)}), bf16[128,32,256]{0,2,1:T(8,128)(2,1)S(1)}, u32[]{:S(2)}, u32[]{:S(2)}) async-start(bf16[128,32,256]{0,2,1:T(8,128)(2,1)} %bitcast.358), calls=%async_computation.1 | async-start | bytes 4194304 | tf_op jit(solution)/shard_map/all_to_all | solution.py:95
  37.8 187.2 %all-gather.7.cloned.1.call-start = ((), (), s32[]{:S(2)}) async-start(), calls=%async_computation.7 | async-start | bytes 4325376 | tf_op jit(solution)/shard_map/all_gather | solution.py:101
  94.4 1.3 copy-start
  94.4 7.0 copy-start.6
  94.4 7.7 copy-start.4
  95.7 62.1 %all-to-all-start.2 = ((bf16[128,32,256]{0,2,1:T(8,128)(2,1)}), bf16[128,32,256]{0,2,1:T(8,128)(2,1)S(1)}, u32[]{:S(2)}, u32[]{:S(2)}) async-start(bf16[128,32,256]{0,2,1:T(8,128)(2,1)} %bitcast.357), calls=%async_computation.2 | async-start | bytes 4194304 | tf_op jit(solution)/shard_map/all_to_all | solution.py:96
  677.4 13.4 %copy-start.2 = (bf16[16,256,128]{2,1,0:T(8,128)(2,1)S(1)}, bf16[16,256,128]{2,1,0:T(8,128)(2,1)}, u32[]{:S(2)}) copy-start(bf16[16,256,128]{2,1,0:T(8,128)(2,1)} %get-tuple-element.311) | copy-start | bytes 3145732
  686.2 14.0 %all-to-all-start.5 = ((bf16[32,2,256]{2,1,0:T(2,128)(2,1)}), bf16[32,2,256]{2,1,0:T(2,128)(2,1)S(1)}, u32[]{:S(2)}, u32[]{:S(2)}) async-start(bf16[32,2,256]{2,1,0:T(2,128)(2,1)} %reshape.421), calls=%async_computation.5 | async-start | bytes 65536 | tf_op jit(solution)/shard_map/all_to_all | solution.py:124
  700.2 32.4 %all-to-all-start.4 = ((bf16[32,2,8192]{2,1,0:T(2,128)(2,1)}), bf16[32,2,8192]{2,1,0:T(2,128)(2,1)S(1)}, u32[]{:S(2)}, u32[]{:S(2)}) async-start(bf16[32,2,8192]{2,1,0:T(2,128)(2,1)} %reshape.419), calls=%async_computation.4 | async-start | bytes 2097152 | tf_op jit(solution)/shard_map/all_to_all | solution.py:121
  732.6 62.3 %all-to-all-start.3 = ((bf16[32,2,8192]{2,1,0:T(2,128)(2,1)}), bf16[32,2,8192]{2,1,0:T(2,128)(2,1)}, u32[]{:S(2)}, u32[]{:S(2)}) async-start(bf16[32,2,8192]{2,1,0:T(2,128)(2,1)} %reshape.417), calls=%async_computation.3 | async-start | bytes 2097152 | tf_op jit(solution)/shard_map/all_to_all | solution.py:118
  746.1 4.3 copy-start.1
  750.5 2.3 copy-start.3
  750.5 2.3 copy-start.5
  750.5 2.6 copy-start.7
Sparse Core Ops, SparseCore 0:
  11.4 120.1 all-gather.4
  134.9 90.1 all-gather.6
where the time goes:
time: 826 us; the launch traced here: 812 us
  local copies, waits for them, and re-layouts  247 us (30%)
  other arithmetic  194 us (23%)
  waiting for transfers between devices  186 us (23%)
  matrix products  100 us (12%)
  starting transfers between devices  40.6 us (5%)
  blocking collectives  28.1 us (3%)
  between operations  14.3 us (2%)
    another operation x128, other arithmetic  124 us
    all_gather x1, waiting for transfers between devices, local(): lax.all_gather(c_proj[0], 'ctx', axis=0, tiled=True)  57.2 us
    squeeze x64, local copies, waits for them, and re-layouts, objective(): lax.scan(stepper, start, (x_heads.reshape(blocks, block, head_count, HEAD...  55.2 us
    all_to_all x1, waiting for transfers between devices, local(): lax.all_to_all(x_split, 'ctx', split_axis=1, concat_axis=0, tiled=True)  51.7 us
    dynamic_slice x64, local copies, waits for them, and re-layouts, objective(): lax.scan(stepper, start, (x_heads.reshape(blocks, block, head_count, HEAD...  45 us
    all_to_all x1, waiting for transfers between devices, local(): lax.all_to_all(grad_split, 'ctx', split_axis=1, concat_axis=0, tiled=True)  42.9 us
    unnamed x32, local copies, waits for them, and re-layouts  39 us
    dot_general x48, matrix products, product(): return jnp.einsum(form, left, right, preferred_element_type=jnp.float32)  38.5 us
  transfers between devices with their start and end apart: 8, of which 6 were waited for; matrix products, arithmetic and copies ran while one was open for 9% of the time, Pallas kernels for 0%

commit v1 on v0

v1 whole, which is shorter than its diff:
```python
from functools import partial

import jax
import jax.numpy as jnp
from jax import lax
from jax.experimental import pallas as pl
from jax.experimental.pallas import tpu as pltpu
from jax.sharding import PartitionSpec as P

HEADDIM = 64
STATE = 128
LANES = 128
WIDE = 512
SKEW = 5
F32 = jnp.float32
BF16 = jnp.bfloat16
MESH = pl.DeviceIdType.MESH


def mm(a, b):
    return lax.dot_general(a, b, (((1,), (0,)), ((), ())), preferred_element_type=F32)


def mm_nt(a, b):
    return lax.dot_general(a, b, (((1,), (1,)), ((), ())), preferred_element_type=F32)


def mm_exact(a, b):
    return lax.dot_general(
        a, b, (((1,), (0,)), ((), ())), precision=lax.Precision.HIGHEST, preferred_element_type=F32
    )


def halves(v):
    high = v.astype(BF16)
    return high, (v - high.astype(F32)).astype(BF16)


def pack(v):
    return (v * jnp.abs(v)).astype(BF16)


def unpack(code):
    u = code.astype(F32)
    root = jnp.sqrt(jnp.abs(u))
    return jnp.where(u < 0.0, -root, root)


def kernel(
    chips, copies_dp, x, g, b, c, raw, par,
    gb, gc, gs, gp,
    xs, gr, bs, cs, rs,
    eh, fh, eg, fx, eg_low, fx_low, fresh, back, s_in, t_in, send_f, send_b, recv_f, recv_b, scale,
    gram, mix, mixt, bt, ct, row, col, dcs, dbs, skip_l, tail_l, draw_s, draw_r,
    par_r, sum_s, sum_r, all_s, all_r,
    own_sem, pair_send, pair_recv, fs_sem, fr_sem, bs_sem, br_sem, out_send, out_recv,
    ps_sem, pr_sem, ss_sem, sr_sem, as_sem, ar_sem,
):
    me = lax.axis_index("ctx")
    me_dp = lax.axis_index("dp")
    core = lax.rem(me, 2)
    pos = lax.div(me, 2)
    count = 2 * chips
    partner = me + 1 - 2 * core
    after = lax.rem(me + 2, count)
    before = lax.rem(me + count - 2, count)
    tok = x.shape[0]
    rows = 2 * tok
    half = xs.shape[1]
    cols = bs.shape[1]
    groups = cols // STATE
    steps = half // WIDE
    per_group = steps // groups
    heads_w = WIDE // HEADDIM
    pieces = half // LANES
    sub = WIDE // LANES
    first_head = core * (half // HEADDIM)
    my_half = lax.div(me, chips)
    my_place = lax.rem(me, chips)

    mine_rows = pl.ds(pl.multiple_of(core * tok, tok), tok)
    their_rows = pl.ds(pl.multiple_of((1 - core) * tok, tok), tok)
    mine_b = pl.ds(pl.multiple_of(core * cols, cols), cols)
    their_b = pl.ds(pl.multiple_of((1 - core) * cols, cols), cols)

    def lanes_of(q):
        return pl.ds(pl.multiple_of(q * WIDE, WIDE), WIDE)

    def moves_of(q):
        mine = pl.ds(pl.multiple_of(core * half + q * WIDE, WIDE), WIDE)
        theirs = pl.ds(pl.multiple_of((1 - core) * half + q * WIDE, WIDE), WIDE)
        return [
            (x.at[:, mine], x.at[:, theirs], xs.at[mine_rows, lanes_of(q)], 3 + 2 * q),
            (g.at[:, mine], g.at[:, theirs], gr.at[mine_rows, lanes_of(q)], 4 + 2 * q),
        ]

    small_moves = [
        (raw, raw, rs.at[mine_rows], 0),
        (b.at[:, mine_b], b.at[:, their_b], bs.at[mine_rows], 1),
        (c.at[:, mine_b], c.at[:, their_b], cs.at[mine_rows], 2),
    ]

    def own_copy(move):
        return pltpu.make_async_copy(move[0], move[2], own_sem.at[move[3]])

    def pair_copy(move):
        return pltpu.make_async_remote_copy(
            src_ref=move[1], dst_ref=move[2],
            send_sem=pair_send.at[move[3]], recv_sem=pair_recv.at[move[3]],
            device_id={"ctx": partner}, device_id_type=MESH,
        )

    for move in small_moves:
        own_copy(move).start()

    def start_own(q, carry):
        for move in moves_of(q):
            own_copy(move).start()
        return carry

    lax.fori_loop(0, steps, start_own, 0)

    barrier = pltpu.get_barrier_semaphore()

    def greet(d, carry):
        pl.semaphore_signal(
            barrier, inc=1, device_id={"ctx": lax.rem(me + d, count)}, device_id_type=MESH
        )
        return carry

    def greet_dp(d, carry):
        pl.semaphore_signal(
            barrier, inc=1, device_id={"dp": lax.rem(me_dp + d, copies_dp)}, device_id_type=MESH
        )
        return carry

    lax.fori_loop(1, count, greet, 0)
    lax.fori_loop(1, copies_dp, greet_dp, 0)
    pl.semaphore_wait(barrier, count - 1 + copies_dp - 1)

    def par_copy(j, place):
        return pltpu.make_async_remote_copy(
            src_ref=par, dst_ref=par_r.at[place], send_sem=ps_sem.at[j], recv_sem=pr_sem.at[place],
            device_id={"ctx": 2 * j + my_half}, device_id_type=MESH,
        )

    def par_send(j, carry):
        @pl.when(2 * j + my_half != me)
        def _():
            par_copy(j, my_place).start()

        return carry

    lax.fori_loop(0, chips, par_send, 0)

    for move in small_moves:
        pair_copy(move).start()

    def start_pair(q, carry):
        for move in moves_of(q):
            pair_copy(move).start()
        return carry

    lax.fori_loop(0, steps, start_pair, 0)

    gram[...] = jnp.zeros_like(gram)
    row[...] = jnp.zeros_like(row)
    col[...] = jnp.zeros_like(col)
    dcs[...] = jnp.zeros_like(dcs)
    dbs[...] = jnp.zeros_like(dbs)

    @pl.when(pos == 0)
    def _():
        recv_f[...] = jnp.zeros_like(recv_f)

    @pl.when(pos == chips - 1)
    def _():
        recv_b[...] = jnp.zeros_like(recv_b)

    for move in small_moves:
        own_copy(move).wait()
        pair_copy(move).wait()

    i_at = lax.broadcasted_iota(jnp.int32, (rows, rows), 0)
    j_at = lax.broadcasted_iota(jnp.int32, (rows, rows), 1)
    causal = i_at >= j_at
    for at in range(groups):
        span = slice(at * STATE, (at + 1) * STATE)
        b_at = bs[:, span]
        c_at = cs[:, span]
        bt[at] = b_at.astype(F32).T.astype(BF16)
        ct[at] = c_at.astype(F32).T.astype(BF16)
        scores = jnp.where(causal, mm_nt(c_at, b_at), 0.0)
        mix[at] = scores.astype(BF16)
        mixt[at] = scores.T.astype(BF16)

    @pl.when(my_half == core)
    def _():
        par_r[my_place] = par[...]

    def par_wait(j, carry):
        @pl.when(chips * core + j != me)
        def _():
            par_copy(j, j).wait_recv()

        return carry

    lax.fori_loop(0, chips, par_wait, 0)

    def step_sizes():
        params = jnp.sum(par_r[...], axis=0)
        z = rs[...].astype(F32) + params[0:1, :]
        dt = jnp.maximum(z, 0.0) + jnp.log1p(jnp.exp(-jnp.abs(z)))
        lane = lax.broadcasted_iota(jnp.int32, (1, z.shape[1]), 1)
        own = lax.div(lane, z.shape[1] // 2) == core
        return z, dt, jnp.where(own, -jnp.exp(params[1:2, :]), 0.0)

    z, dt, rate = step_sizes()
    cum = mm_exact(causal.astype(F32), dt * rate)
    mid = cum[rows - 1 : rows, :] * 0.5
    e_hi, e_lo = halves(jnp.exp(cum - mid))
    f_hi, f_lo = halves(jnp.exp(mid - cum) * dt)
    eh[:, :LANES] = e_hi
    eh[:, LANES:] = e_lo
    fh[:, :LANES] = f_hi
    fh[:, LANES:] = f_lo
    a_hi, a_lo = halves(jnp.broadcast_to(jnp.exp(mid), (16, LANES)))
    a_both = jnp.concatenate([a_hi, a_lo], axis=1)

    def spread_of(q):
        head = lax.broadcasted_iota(jnp.int32, (LANES, WIDE), 0)
        lane = lax.broadcasted_iota(jnp.int32, (LANES, WIDE), 1)
        return (head == first_head + q * heads_w + lax.div(lane, HEADDIM)).astype(F32).astype(BF16)

    def fold(v, spread):
        high, low = halves(v)
        return mm_nt(high, spread) + mm_nt(low, spread)

    def full(high, low, here):
        return high[:, here].astype(F32) + low[:, here].astype(F32)

    def dense(q):
        for move in moves_of(q):
            own_copy(move).wait()
            pair_copy(move).wait()
        at = lax.div(q, per_group)
        here = lanes_of(q)
        spread = spread_of(q)
        both = jnp.concatenate([spread, spread], axis=0)
        x_q = xs[:, here].astype(F32)
        g_q = gr[:, here].astype(F32)
        skip_l[0:1, here] = jnp.sum(x_q * g_q, axis=0, keepdims=True)
        eg_q, eg_rest = halves(mm(eh[...], both) * g_q)
        fx_q, fx_rest = halves(mm(fh[...], both) * x_q)
        eg[:, here] = eg_q
        fx[:, here] = fx_q
        eg_low[:, here] = eg_rest
        fx_low[:, here] = fx_rest
        fresh_q = mm(bt[at], fx_q) + mm(bt[at], fx_rest)
        back_q = mm(ct[at], eg_q) + mm(ct[at], eg_rest)
        scale_q = mm(a_both, both)
        for k in range(sub):
            span = slice(k * LANES, (k + 1) * LANES)
            fresh[q * sub + k] = fresh_q[:, span]
            back[q * sub + k] = back_q[:, span]
            scale[q * sub + k] = scale_q[0:8, span]

    def inner(q):
        at = lax.div(q, per_group)
        here = lanes_of(q)
        spread = spread_of(q)
        eg_q = eg[:, here]
        fx_q = fx[:, here]
        gram[at] += mm_nt(eg_q, fx_q)
        y_q = mm(mix[at], fx_q) + mm(mix[at], fx_low[:, here])
        v_q = mm(mixt[at], eg_q) + mm(mixt[at], eg_low[:, here])
        row[...] += fold(full(eg, eg_low, here) * y_q, spread)
        col[...] += fold(full(fx, fx_low, here) * v_q, spread)

    def cross():
        for at in range(groups):
            span = slice(at * STATE, (at + 1) * STATE)
            cot = jnp.where(causal, gram[at], 0.0)
            dcs[:, span] += mm(cot.astype(BF16), bs[:, span])
            dbs[:, span] += mm(cot.T.astype(BF16), cs[:, span])

    def outer(q):
        at = lax.div(q, per_group)
        here = lanes_of(q)
        span = pl.ds(pl.multiple_of(at * STATE, STATE), STATE)
        spread = spread_of(q)
        s_q = jnp.concatenate([s_in[q * sub + k] for k in range(sub)], axis=1)
        t_q = jnp.concatenate([t_in[q * sub + k] for k in range(sub)], axis=1)
        f_q = jnp.concatenate([fresh[q * sub + k] for k in range(sub)], axis=1)
        row[...] += fold(full(eg, eg_low, here) * mm(cs[:, span], s_q), spread)
        col[...] += fold(full(fx, fx_low, here) * mm(bs[:, span], t_q), spread)
        dcs[:, span] += mm_nt(eg[:, here], s_q)
        dbs[:, span] += mm_nt(fx[:, here], t_q)
        whole = (s_q.astype(F32) + f_q) * t_q.astype(F32)
        tail_l[0:1, here] = jnp.sum(whole, axis=0, keepdims=True)

    def up(k):
        return pltpu.make_async_remote_copy(
            src_ref=send_f.at[k], dst_ref=recv_f.at[k], send_sem=fs_sem.at[k], recv_sem=fr_sem.at[k],
            device_id={"ctx": after}, device_id_type=MESH,
        )

    def down(k):
        return pltpu.make_async_remote_copy(
            src_ref=send_b.at[k], dst_ref=recv_b.at[k], send_sem=bs_sem.at[k], recv_sem=br_sem.at[k],
            device_id={"ctx": before}, device_id_type=MESH,
        )

    far = (chips - 1) * SKEW
    near = jnp.minimum(pos, chips - 1 - pos)
    inner_from = jnp.where(near >= chips // 4, 2, near * SKEW + pieces)
    inner_from = jnp.minimum(inner_from, far + sub - 1)

    def slot(t, carry):
        k_f = t - pos * SKEW
        k_b = t - (chips - 1 - pos) * SKEW

        @pl.when((t < sub * steps) & (lax.rem(t, sub) == 0))
        def _():
            dense(lax.div(t, sub))

        @pl.when((k_f >= 0) & (k_f < pieces))
        def _():
            @pl.when(pos > 0)
            def _():
                up(k_f).wait_recv()

            by = scale[k_f][0:1, :]
            entering = by * unpack(recv_f[k_f])
            s_in[k_f] = entering.astype(BF16)

            @pl.when(pos < chips - 1)
            def _():
                send_f[k_f] = pack(by * (entering + fresh[k_f]))
                up(k_f).start()

        @pl.when((k_b >= 0) & (k_b < pieces))
        def _():
            @pl.when(pos < chips - 1)
            def _():
                down(k_b).wait_recv()

            by = scale[k_b][0:1, :]
            entering = by * unpack(recv_b[k_b])
            t_in[k_b] = entering.astype(BF16)

            @pl.when(pos > 0)
            def _():
                send_b[k_b] = pack(by * (entering + back[k_b]))
                down(k_b).start()

        k_i = t - inner_from

        @pl.when((k_i >= 0) & (k_i < sub * steps) & (lax.rem(k_i, sub) == 0))
        def _():
            inner(lax.div(k_i, sub))

        @pl.when(k_i == sub * steps)
        def _():
            cross()

        k_o = t - far - sub

        @pl.when((k_o >= 0) & (lax.rem(k_o, sub) == 0))
        def _():
            outer(lax.div(k_o, sub))

        return carry

    lax.fori_loop(0, far + sub + pieces, slot, 0)

    def gather_rows(q, carry):
        spread = spread_of(q)
        here = lanes_of(q)
        tail_q = fold(jnp.broadcast_to(tail_l[0:1, here], (16, WIDE)), spread)
        skip_q = fold(jnp.broadcast_to(skip_l[0:1, here], (16, WIDE)), spread)
        return (carry[0] + tail_q[0:1, :], carry[1] + skip_q[0:1, :])

    zero = jnp.zeros((1, LANES), F32)
    d_tail, d_skip = lax.fori_loop(0, steps, gather_rows, (zero, zero))

    z, dt, rate = step_sizes()
    d_a = d_tail + mm_exact((i_at <= j_at).astype(F32), row[...] - col[...])
    d_dt = col[...] / dt + rate * d_a
    d_raw = d_dt * jax.nn.sigmoid(z)
    sum_s[...] = jnp.zeros_like(sum_s)
    sum_s[0:1, :] = rate * jnp.sum(d_a * dt, axis=0, keepdims=True)
    sum_s[1:2, :] = jnp.sum(d_raw, axis=0, keepdims=True)
    sum_s[2:3, :] = d_skip
    draw_s[...] = d_raw

    def sum_copy(j, place):
        return pltpu.make_async_remote_copy(
            src_ref=sum_s, dst_ref=sum_r.at[place], send_sem=ss_sem.at[j], recv_sem=sr_sem.at[place],
            device_id={"ctx": chips * core + j}, device_id_type=MESH,
        )

    def sum_send(j, carry):
        @pl.when(chips * core + j != me)
        def _():
            sum_copy(j, pos).start()

        return carry

    lax.fori_loop(0, chips, sum_send, 0)

    backs = [
        (dbs.at[their_rows], gb.at[:, mine_b]),
        (dcs.at[their_rows], gc.at[:, mine_b]),
        (draw_s.at[their_rows], draw_r),
    ]
    copies = []
    for at, (src, dst) in enumerate(backs):
        copy = pltpu.make_async_remote_copy(
            src_ref=src, dst_ref=dst, send_sem=out_send.at[at], recv_sem=out_recv.at[at],
            device_id={"ctx": partner}, device_id_type=MESH,
        )
        copy.start()
        copies.append(copy)
    gb[:, mine_b] = dbs[mine_rows, :]
    gc[:, mine_b] = dcs[mine_rows, :]

    @pl.when(my_half == core)
    def _():
        sum_r[pos] = sum_s[...]

    def sum_wait(j, carry):
        @pl.when(2 * j + my_half != me)
        def _():
            sum_copy(j, j).wait_recv()

        return carry

    lax.fori_loop(0, chips, sum_wait, 0)
    total = jnp.sum(sum_r[...], axis=0)
    all_s[...] = total

    def all_copy(d, place):
        return pltpu.make_async_remote_copy(
            src_ref=all_s, dst_ref=all_r.at[place], send_sem=as_sem.at[d], recv_sem=ar_sem.at[place],
            device_id={"dp": lax.rem(me_dp + d, copies_dp)}, device_id_type=MESH,
        )

    def all_send(d, carry):
        all_copy(d, d).start()
        return carry

    def all_wait(d, carry):
        all_copy(d, d).wait()
        return carry

    lax.fori_loop(1, copies_dp, all_send, 0)

    def drain(k, carry):
        @pl.when(pos < chips - 1)
        def _():
            up(k).wait_send()

        @pl.when(pos > 0)
        def _():
            down(k).wait_send()

        return carry

    lax.fori_loop(0, pieces, drain, 0)

    def drain_small(j, carry):
        @pl.when(2 * j + my_half != me)
        def _():
            par_copy(j, my_place).wait_send()

        @pl.when(chips * core + j != me)
        def _():
            sum_copy(j, pos).wait_send()

        return carry

    lax.fori_loop(0, chips, drain_small, 0)
    for copy in copies:
        copy.wait()
    gs[...] = (draw_s[mine_rows, :] + draw_r[...]).astype(BF16)
    lax.fori_loop(1, copies_dp, all_wait, 0)
    all_r[0] = total
    heads = total.shape[1]
    span = heads // count
    head = lax.broadcasted_iota(jnp.int32, (heads, heads), 0)
    lane = lax.broadcasted_iota(jnp.int32, (heads, heads), 1)
    pick = ((head == me * span + lane) & (lane < span)).astype(F32)
    gp[...] = mm_exact(jnp.sum(all_r[...], axis=0), pick)


def run(x, g, b, c, raw, par, chips, copies_dp):
    tok, wide = x.shape
    half = wide // 2
    cols = b.shape[1] // 2
    groups = cols // STATE
    rows = 2 * tok
    pieces = half // LANES
    heads = raw.shape[1]
    steps = half // WIDE
    anywhere = pl.BlockSpec(memory_space=pl.ANY)
    inside = pl.BlockSpec(memory_space=pltpu.VMEM)
    state16 = pltpu.VMEM((pieces, STATE, LANES), BF16)
    state32 = pltpu.VMEM((pieces, STATE, LANES), F32)
    wide16 = pltpu.VMEM((rows, half), BF16)
    tile = pltpu.VMEM((8, heads), F32)
    dma = pltpu.SemaphoreType.DMA
    moves = 3 + 2 * steps
    return pl.pallas_call(
        partial(kernel, chips, copies_dp),
        out_shape=(
            jax.ShapeDtypeStruct((tok, 2 * cols), F32),
            jax.ShapeDtypeStruct((tok, 2 * cols), F32),
            jax.ShapeDtypeStruct((tok, heads), BF16),
            jax.ShapeDtypeStruct((8, heads), F32),
        ),
        in_specs=[anywhere] * 5 + [inside],
        out_specs=(inside,) * 4,
        scratch_shapes=[
            wide16, wide16,
            pltpu.VMEM((rows, cols), BF16), pltpu.VMEM((rows, cols), BF16),
            pltpu.VMEM((rows, heads), BF16),
            pltpu.VMEM((rows, 2 * LANES), BF16), pltpu.VMEM((rows, 2 * LANES), BF16),
            wide16, wide16, wide16, wide16,
            state32, state32, state16, state16, state16, state16, state16, state16,
            pltpu.VMEM((pieces, 8, LANES), F32),
            pltpu.VMEM((groups, rows, rows), F32),
            pltpu.VMEM((groups, rows, rows), BF16), pltpu.VMEM((groups, rows, rows), BF16),
            pltpu.VMEM((groups, STATE, rows), BF16), pltpu.VMEM((groups, STATE, rows), BF16),
            pltpu.VMEM((rows, LANES), F32), pltpu.VMEM((rows, LANES), F32),
            pltpu.VMEM((rows, cols), F32), pltpu.VMEM((rows, cols), F32),
            pltpu.VMEM((8, half), F32), pltpu.VMEM((8, half), F32),
            pltpu.VMEM((rows, heads), F32), pltpu.VMEM((tok, heads), F32),
            pltpu.VMEM((chips, 8, heads), F32),
            tile, pltpu.VMEM((chips, 8, heads), F32),
            tile, pltpu.VMEM((copies_dp, 8, heads), F32),
            dma((moves,)), dma((moves,)), dma((moves,)),
            dma((pieces,)), dma((pieces,)), dma((pieces,)), dma((pieces,)),
            dma((3,)), dma((3,)),
            dma((chips,)), dma((chips,)), dma((chips,)), dma((chips,)),
            dma((copies_dp,)), dma((copies_dp,)),
        ],
        compiler_params=pltpu.CompilerParams(
            collective_id=0, has_side_effects=True, vmem_limit_bytes=60 * 1024 * 1024
        ),
        name="scan_backward",
    )(x, g, b, c, raw, par)


def local(x_tokens, grad_out, step_raw, step_bias, decay_log, b_proj, c_proj):
    shards = lax.axis_size("ctx")
    me = lax.axis_index("ctx")
    span = step_bias.shape[0]
    mine = lax.broadcasted_iota(jnp.int32, (8, span * shards), 1) // span == me
    pair = jnp.tile(jnp.stack([step_bias, decay_log]), (4, shards))
    par = jnp.where(mine, pair, 0.0)
    gb, gc, gs, gp = run(
        x_tokens[0], grad_out[0], b_proj[0], c_proj[0], step_raw[0], par,
        shards // 2, lax.axis_size("dp"),
    )
    return (gb[None], gc[None], gs[None], gp[0, :span], gp[1, :span], gp[2, :span])


def solution(mesh):
    tokens = P("dp", "ctx", None)
    return jax.shard_map(
        local,
        mesh=mesh,
        in_specs=(tokens, tokens, tokens, P("ctx"), P("ctx"), tokens, tokens),
        out_specs=(tokens, tokens, tokens, P("ctx"), P("ctx"), P("ctx")),
        check_vma=False,
    )
```

time: 826 us -> 127 us (0.15); the launches traced: 812 us -> 127 us
  local copies, waits for them, and re-layouts: 247 us -> 6.15 us
  other arithmetic: 194 us -> 1.3 us
  waiting for transfers between devices: 186 us -> 0 us
  Pallas kernels: 0 us -> 119 us
  matrix products: 100 us -> 0 us
  starting transfers between devices: 40.6 us -> 0 us
  blocking collectives: 28.1 us -> 0 us
  between operations: 14.3 us -> 0.66 us
    all_to_all x6 -> x0, waiting for transfers between devices: 127 us -> none  [the longest x1 51.7 us: local(): lax.all_to_all(x_split, 'ctx', split_axis=1, concat_axis=0, tiled=True)]
    another operation x144 -> x1, other arithmetic: 124 us -> 0.68 us  [local(): pair = jnp.tile(jnp.stack([step_bias, decay_log]), (4, shards))]
    pallas_call x0 -> x1, Pallas kernels: none -> 119 us  [run(): pl.pallas_call(partial(kernel, chips, copies_dp), out_shape=(jax.ShapeDty...]
    dot_general x128 -> x0, matrix products: 93.9 us -> none  [the longest x48 38.5 us: product(): return jnp.einsum(form, left, right, preferred_element_type=jnp.float32)]
    all_gather x2 -> x0, waiting for transfers between devices: 57.2 us -> none  [the longest x1 57.2 us: local(): lax.all_gather(c_proj[0], 'ctx', axis=0, tiled=True)]
    squeeze x64 -> x1, local copies, waits for them, and re-layouts: 55.2 us -> 1.31 us  [local(): gp[2, :span]]
    dynamic_slice x65 -> x0, local copies, waits for them, and re-layouts: 46.8 us -> none  [the longest x64 45 us: objective(): lax.scan(stepper, start, (x_heads.reshape(blocks, block, head_count, HEAD...]
    all_to_all x6 -> x0, starting transfers between devices: 40.5 us -> none  [the longest x1 14.4 us: local(): lax.all_to_all(raw_split, 'ctx', split_axis=1, concat_axis=0, tiled=True)]
  transfers between devices with their start and end apart: 8 -> 0, of which waited for: 6 -> 0; matrix products, arithmetic and copies ran while one was open for 9% -> 0% of each run, Pallas kernels for 0% -> 0%
where the time goes in v1:
time: 127 us
  Pallas kernels  119 us (94%)
  local copies, waits for them, and re-layouts  6.15 us (5%)
  other arithmetic  1.3 us (1%)
    pallas_call x1, Pallas kernels, run(): pl.pallas_call(partial(kernel, chips, copies_dp), out_shape=(jax.ShapeDty...  119 us
    unnamed x3, local copies, waits for them, and re-layouts  4.71 us

profile of v1, /device:TPU:1, one launch (start us, length us, event | category | flops | bytes accessed | tf_op | source)
XLA Modules:
  0.0 127.2 jit_solution(18100210254550434474)
XLA Ops:
  0.6 0.7 pad_maximum_fusion
  1.3 0.1 tile.10
  1.5 0.6 fusion.par
  2.1 119.1 %scan_backward.1 = (f32[128,512]{1,0:T(8,128)}, f32[128,512]{1,0:T(8,128)}, bf16[128,128]{1,0:T(8,128)(2,1)}, f32[8,128]{1,0:T(8,128)}) custom-call(bf16[128,8192]{1,0:T(8,128)(2,1)} %bitcast.18, bf16[128,8192]{1,0:T(8,128)(2,1)} %bitcast.19, bf16[128,512]{1,0:T(8,128)(2,1)} %bitcast.22, bf16[128,512]{1,0:T(8,128)(2,1)} %bitcast.23, ...), custom_call_target="tpu_custom_call" | custom-call | tf_op jit(solution)/shard_map/scan_backward/pallas_call | solution.py:514
  121.1 1.3 %slice_bitcast_fusion = (f32[4]{0:T(128)}, f32[4]{0:T(128)}, f32[4]{0:T(128)}) fusion(f32[8,128]{1,0:T(8,128)} %get-tuple-element.13), kind=kLoop, calls=%fused_computation.7 | loop fusion | bytes 96 | tf_op jit(solution)/shard_map/squeeze | solution.py:566
  122.5 1.7 %copy.16 = f32[1,128,512]{2,1,0:T(8,128)} copy(f32[1,128,512]{2,1,0:T(8,128)} %bitcast.21) | data formatting | bytes 524288
  124.1 1.7 %copy.17 = f32[1,128,512]{2,1,0:T(8,128)} copy(f32[1,128,512]{2,1,0:T(8,128)} %bitcast.20) | data formatting | bytes 524288
  125.8 1.4 %copy.18 = bf16[1,128,128]{2,1,0:T(8,128)(2,1)} copy(bf16[1,128,128]{2,1,0:T(8,128)(2,1)} %bitcast.25) | data formatting | bytes 65536
  (3 shorter events, 0.0 us)

commit v2 on v1

--- a/solution.py
+++ b/solution.py
@@ -11,7 +11,7 @@
 STATE = 128
 LANES = 128
 WIDE = 512
-SKEW = 5
+SKEW = 7
 F32 = jnp.float32
 BF16 = jnp.bfloat16
 MESH = pl.DeviceIdType.MESH
@@ -47,12 +47,12 @@
 
 
 def kernel(
-    chips, copies_dp, x, g, b, c, raw, par,
+    chips, copies_dp, x, g, b, c, raw, bias, log_rate,
     gb, gc, gs, gp,
     xs, gr, bs, cs, rs,
     eh, fh, eg, fx, eg_low, fx_low, fresh, back, s_in, t_in, send_f, send_b, recv_f, recv_b, scale,
-    gram, mix, mixt, bt, ct, row, col, dcs, dbs, skip_l, tail_l, draw_s, draw_r,
-    par_r, sum_s, sum_r, all_s, all_r,
+    gram, mix, mixt, bt, ct, row, col, dcs, dbs, d_skip, d_tail, draw_s, draw_r,
+    par, par_r, sum_s, sum_r, all_s, all_r,
     own_sem, pair_send, pair_recv, fs_sem, fr_sem, bs_sem, br_sem, out_send, out_recv,
     ps_sem, pr_sem, ss_sem, sr_sem, as_sem, ar_sem,
 ):
@@ -110,6 +110,16 @@
             device_id={"ctx": partner}, device_id_type=MESH,
         )
 
+    held = bias.shape[0]
+    lane = lax.broadcasted_iota(jnp.int32, (8, par.shape[1]), 1)
+    line = lax.broadcasted_iota(jnp.int32, (8, par.shape[1]), 0)
+    tile = jnp.zeros(par.shape, F32)
+    for k in range(held):
+        here = lane == me * held + k
+        tile = jnp.where(here & (line == 0), bias[k], tile)
+        tile = jnp.where(here & (line == 1), log_rate[k], tile)
+    par[...] = tile
+
     for move in small_moves:
         own_copy(move).start()
 
@@ -168,6 +178,8 @@
     col[...] = jnp.zeros_like(col)
     dcs[...] = jnp.zeros_like(dcs)
     dbs[...] = jnp.zeros_like(dbs)
+    d_skip[...] = jnp.zeros_like(d_skip)
+    d_tail[...] = jnp.zeros_like(d_tail)
 
     @pl.when(pos == 0)
     def _():
@@ -236,6 +248,9 @@
         high, low = halves(v)
         return mm_nt(high, spread) + mm_nt(low, spread)
 
+    def fold_line(v, spread):
+        return fold(jnp.broadcast_to(v, (16, WIDE)), spread)[0:8, :]
+
     def full(high, low, here):
         return high[:, here].astype(F32) + low[:, here].astype(F32)
 
@@ -249,7 +264,7 @@
         both = jnp.concatenate([spread, spread], axis=0)
         x_q = xs[:, here].astype(F32)
         g_q = gr[:, here].astype(F32)
-        skip_l[0:1, here] = jnp.sum(x_q * g_q, axis=0, keepdims=True)
+        d_skip[...] += fold_line(jnp.sum(x_q * g_q, axis=0, keepdims=True), spread)
         eg_q, eg_rest = halves(mm(eh[...], both) * g_q)
         fx_q, fx_rest = halves(mm(fh[...], both) * x_q)
         eg[:, here] = eg_q
@@ -297,7 +312,7 @@
         dcs[:, span] += mm_nt(eg[:, here], s_q)
         dbs[:, span] += mm_nt(fx[:, here], t_q)
         whole = (s_q.astype(F32) + f_q) * t_q.astype(F32)
-        tail_l[0:1, here] = jnp.sum(whole, axis=0, keepdims=True)
+        d_tail[...] += fold_line(jnp.sum(whole, axis=0, keepdims=True), spread)
 
     def up(k):
         return pltpu.make_async_remote_copy(
@@ -374,24 +389,14 @@
 
     lax.fori_loop(0, far + sub + pieces, slot, 0)
 
-    def gather_rows(q, carry):
-        spread = spread_of(q)
-        here = lanes_of(q)
-        tail_q = fold(jnp.broadcast_to(tail_l[0:1, here], (16, WIDE)), spread)
-        skip_q = fold(jnp.broadcast_to(skip_l[0:1, here], (16, WIDE)), spread)
-        return (carry[0] + tail_q[0:1, :], carry[1] + skip_q[0:1, :])
-
-    zero = jnp.zeros((1, LANES), F32)
-    d_tail, d_skip = lax.fori_loop(0, steps, gather_rows, (zero, zero))
-
     z, dt, rate = step_sizes()
-    d_a = d_tail + mm_exact((i_at <= j_at).astype(F32), row[...] - col[...])
+    d_a = d_tail[0:1, :] + mm_exact((i_at <= j_at).astype(F32), row[...] - col[...])
     d_dt = col[...] / dt + rate * d_a
     d_raw = d_dt * jax.nn.sigmoid(z)
     sum_s[...] = jnp.zeros_like(sum_s)
     sum_s[0:1, :] = rate * jnp.sum(d_a * dt, axis=0, keepdims=True)
     sum_s[1:2, :] = jnp.sum(d_raw, axis=0, keepdims=True)
-    sum_s[2:3, :] = d_skip
+    sum_s[2:3, :] = d_skip[0:1, :]
     draw_s[...] = d_raw
 
     def sum_copy(j, place):
@@ -487,14 +492,23 @@
     lax.fori_loop(1, copies_dp, all_wait, 0)
     all_r[0] = total
     heads = total.shape[1]
-    span = heads // count
     head = lax.broadcasted_iota(jnp.int32, (heads, heads), 0)
     lane = lax.broadcasted_iota(jnp.int32, (heads, heads), 1)
-    pick = ((head == me * span + lane) & (lane < span)).astype(F32)
+    pick = ((head == me * held + lane) & (lane < held)).astype(F32)
     gp[...] = mm_exact(jnp.sum(all_r[...], axis=0), pick)
 
 
-def run(x, g, b, c, raw, par, chips, copies_dp):
+def finish(gb, gc, gs, gp, gb_out, gc_out, gs_out, decay_out, bias_out, skip_out):
+    gb_out[...] = gb[...]
+    gc_out[...] = gc[...]
+    gs_out[...] = gs[...]
+    span = decay_out.shape[1]
+    decay_out[...] = gp[0:1, :span]
+    bias_out[...] = gp[1:2, :span]
+    skip_out[...] = gp[2:3, :span]
+
+
+def run(x, g, b, c, raw, bias, log_rate, chips, copies_dp):
     tok, wide = x.shape
     half = wide // 2
     cols = b.shape[1] // 2
@@ -505,13 +519,14 @@
     steps = half // WIDE
     anywhere = pl.BlockSpec(memory_space=pl.ANY)
     inside = pl.BlockSpec(memory_space=pltpu.VMEM)
+    scalars = pl.BlockSpec(memory_space=pltpu.SMEM)
     state16 = pltpu.VMEM((pieces, STATE, LANES), BF16)
     state32 = pltpu.VMEM((pieces, STATE, LANES), F32)
     wide16 = pltpu.VMEM((rows, half), BF16)
     tile = pltpu.VMEM((8, heads), F32)
     dma = pltpu.SemaphoreType.DMA
     moves = 3 + 2 * steps
-    return pl.pallas_call(
+    parts = pl.pallas_call(
         partial(kernel, chips, copies_dp),
         out_shape=(
             jax.ShapeDtypeStruct((tok, 2 * cols), F32),
@@ -519,7 +534,7 @@
             jax.ShapeDtypeStruct((tok, heads), BF16),
             jax.ShapeDtypeStruct((8, heads), F32),
         ),
-        in_specs=[anywhere] * 5 + [inside],
+        in_specs=[anywhere] * 5 + [scalars] * 2,
         out_specs=(inside,) * 4,
         scratch_shapes=[
             wide16, wide16,
@@ -534,9 +549,9 @@
             pltpu.VMEM((groups, STATE, rows), BF16), pltpu.VMEM((groups, STATE, rows), BF16),
             pltpu.VMEM((rows, LANES), F32), pltpu.VMEM((rows, LANES), F32),
             pltpu.VMEM((rows, cols), F32), pltpu.VMEM((rows, cols), F32),
-            pltpu.VMEM((8, half), F32), pltpu.VMEM((8, half), F32),
+            tile, tile,
             pltpu.VMEM((rows, heads), F32), pltpu.VMEM((tok, heads), F32),
-            pltpu.VMEM((chips, 8, heads), F32),
+            tile, pltpu.VMEM((chips, 8, heads), F32),
             tile, pltpu.VMEM((chips, 8, heads), F32),
             tile, pltpu.VMEM((copies_dp, 8, heads), F32),
             dma((moves,)), dma((moves,)), dma((moves,)),
@@ -549,21 +564,24 @@
             collective_id=0, has_side_effects=True, vmem_limit_bytes=60 * 1024 * 1024
         ),
         name="scan_backward",
-    )(x, g, b, c, raw, par)
+    )(x, g, b, c, raw, bias, log_rate)
+    line = jax.ShapeDtypeStruct((1, bias.shape[0]), F32)
+    return pl.pallas_call(
+        finish,
+        out_shape=tuple(jax.ShapeDtypeStruct(v.shape, v.dtype) for v in parts[:3]) + (line,) * 3,
+        in_specs=[inside] * 4,
+        out_specs=(inside,) * 6,
+        compiler_params=pltpu.CompilerParams(vmem_limit_bytes=60 * 1024 * 1024),
+        name="results",
+    )(*parts)
 
 
 def local(x_tokens, grad_out, step_raw, step_bias, decay_log, b_proj, c_proj):
-    shards = lax.axis_size("ctx")
-    me = lax.axis_index("ctx")
-    span = step_bias.shape[0]
-    mine = lax.broadcasted_iota(jnp.int32, (8, span * shards), 1) // span == me
-    pair = jnp.tile(jnp.stack([step_bias, decay_log]), (4, shards))
-    par = jnp.where(mine, pair, 0.0)
-    gb, gc, gs, gp = run(
-        x_tokens[0], grad_out[0], b_proj[0], c_proj[0], step_raw[0], par,
-        shards // 2, lax.axis_size("dp"),
+    gb, gc, gs, decay, bias, skip = run(
+        x_tokens[0], grad_out[0], b_proj[0], c_proj[0], step_raw[0], step_bias, decay_log,
+        lax.axis_size("ctx") // 2, lax.axis_size("dp"),
     )
-    return (gb[None], gc[None], gs[None], gp[0, :span], gp[1, :span], gp[2, :span])
+    return (gb[None], gc[None], gs[None], decay[0], bias[0], skip[0])
 
 
 def solution(mesh):

time: 127 us -> 116 us (0.913)
  local copies, waits for them, and re-layouts: 6.15 us -> 0 us
  Pallas kernels: 119 us -> 115 us
  other arithmetic: 1.3 us -> 0 us
    pallas_call x1, Pallas kernels: 119 us -> 113 us  [run(): pl.pallas_call(partial(kernel, chips, copies_dp), out_shape=(jax.ShapeDty...]
    unnamed x3 -> x0, local copies, waits for them, and re-layouts: 4.71 us -> none
    pallas_call x0 -> x1, Pallas kernels: none -> 1.85 us  [run(): pl.pallas_call(finish, out_shape=tuple((jax.ShapeDtypeStruct(v.shape, v.d...]
    squeeze x1 -> x0, local copies, waits for them, and re-layouts: 1.31 us -> none  [local(): gp[2, :span]]
where the time goes in v2:
time: 116 us
  Pallas kernels  115 us (99%)
    pallas_call x1, Pallas kernels, run(): pl.pallas_call(partial(kernel, chips, copies_dp), out_shape=(jax.ShapeDty...  113 us

profile of v2, /device:TPU:1, one launch (start us, length us, event | category | flops | bytes accessed | tf_op | source)
XLA Modules:
  0.0 115.8 jit_solution(18212562965911143289)
XLA Ops:
  0.6 113.3 %scan_backward.1 = (f32[128,512]{1,0:T(8,128)}, f32[128,512]{1,0:T(8,128)}, bf16[128,128]{1,0:T(8,128)(2,1)}, f32[8,128]{1,0:T(8,128)}) custom-call(bf16[128,8192]{1,0:T(8,128)(2,1)} %bitcast.11, bf16[128,8192]{1,0:T(8,128)(2,1)} %bitcast.12, bf16[128,512]{1,0:T(8,128)(2,1)} %bitcast.13, bf16[128,512]{1,0:T(8,128)(2,1)} %bitcast.14, ...), custom_call_target="tpu_custom_call" | custom-call | tf_op jit(solution)/shard_map/scan_backward/pallas_call | solution.py:529
  113.9 1.9 %results.1 = (f32[128,512]{1,0:T(8,128)}, f32[128,512]{1,0:T(8,128)}, bf16[128,128]{1,0:T(8,128)(2,1)}, f32[1,4]{1,0:T(1,128)}, f32[1,4]{1,0:T(1,128)}, /*index=5*/f32[1,4]{1,0:T(1,128)}) custom-call(f32[128,512]{1,0:T(8,128)} %get-tuple-element.16.gb, f32[128,512]{1,0:T(8,128)} %get-tuple-element.17.gc, bf16[128,128]{1,0:T(8,128)(2,1)} %get-tuple-element.18.gs, ...), custom_call_target="tpu_custom_call" | custom-call | tf_op jit(solution)/shard_map/results/pallas_call | solution.py:569

commit v3 on v2

--- a/solution.py
+++ b/solution.py
@@ -11,7 +11,8 @@
 STATE = 128
 LANES = 128
 WIDE = 512
-SKEW = 7
+SKEW = 5
+DELAY = 12
 F32 = jnp.float32
 BF16 = jnp.bfloat16
 MESH = pl.DeviceIdType.MESH
@@ -25,15 +26,16 @@
     return lax.dot_general(a, b, (((1,), (1,)), ((), ())), preferred_element_type=F32)
 
 
-def mm_exact(a, b):
-    return lax.dot_general(
-        a, b, (((1,), (0,)), ((), ())), precision=lax.Precision.HIGHEST, preferred_element_type=F32
-    )
-
-
 def halves(v):
     high = v.astype(BF16)
     return high, (v - high.astype(F32)).astype(BF16)
+
+
+def thirds(v):
+    high = v.astype(BF16)
+    rest = v - high.astype(F32)
+    middle = rest.astype(BF16)
+    return high, middle, (rest - middle.astype(F32)).astype(BF16)
 
 
 def pack(v):
@@ -50,10 +52,12 @@
     chips, copies_dp, x, g, b, c, raw, bias, log_rate,
     gb, gc, gs, gp,
     xs, gr, bs, cs, rs,
-    eh, fh, eg, fx, eg_low, fx_low, fresh, back, s_in, t_in, send_f, send_b, recv_f, recv_b, scale,
-    gram, mix, mixt, bt, ct, row, col, dcs, dbs, d_skip, d_tail, draw_s, draw_r,
+    eh, fh, eg, fx, eg_low, fx_low, fresh, back, send_f, send_b, recv_f, recv_b, recv_e, kept, scale,
+    decay, past_s, past_r,
+    gram, mix, mixt, bt, ct, row, col, dcs, dbs, d_skip, d_tail, draw_s, draw_r, gs_v,
     par, par_r, sum_s, sum_r, all_s, all_r,
-    own_sem, pair_send, pair_recv, fs_sem, fr_sem, bs_sem, br_sem, out_send, out_recv,
+    own_sem, pair_send, pair_recv, fs_sem, fr_sem, bs_sem, br_sem, er_sem, ea_sem, eb_sem,
+    past_sem, out_send, out_recv,
     ps_sem, pr_sem, ss_sem, sr_sem, as_sem, ar_sem,
 ):
     me = lax.axis_index("ctx")
@@ -62,8 +66,17 @@
     pos = lax.div(me, 2)
     count = 2 * chips
     partner = me + 1 - 2 * core
-    after = lax.rem(me + 2, count)
-    before = lax.rem(me + count - 2, count)
+    run_len = chips // 2
+    side = lax.div(pos, run_len)
+    loc = lax.rem(pos, run_len)
+    depth = jnp.where(side == 1, loc, run_len - 1 - loc)
+
+    def chip_at(run, at):
+        return (run * run_len + at) * 2 + core
+
+    def at_depth(d):
+        return chip_at(side, jnp.where(side == 1, d, run_len - 1 - d))
+
     tok = x.shape[0]
     rows = 2 * tok
     half = xs.shape[1]
@@ -181,13 +194,17 @@
     d_skip[...] = jnp.zeros_like(d_skip)
     d_tail[...] = jnp.zeros_like(d_tail)
 
-    @pl.when(pos == 0)
+    @pl.when(loc == 0)
     def _():
         recv_f[...] = jnp.zeros_like(recv_f)
 
-    @pl.when(pos == chips - 1)
+    @pl.when(loc == run_len - 1)
     def _():
         recv_b[...] = jnp.zeros_like(recv_b)
+
+    @pl.when(depth == 0)
+    def _():
+        past_r[...] = jnp.ones_like(past_r)
 
     for move in small_moves:
         own_copy(move).wait()
@@ -228,7 +245,8 @@
         return z, dt, jnp.where(own, -jnp.exp(params[1:2, :]), 0.0)
 
     z, dt, rate = step_sizes()
-    cum = mm_exact(causal.astype(F32), dt * rate)
+    ones = causal.astype(F32).astype(BF16)
+    cum = sum(mm(ones, part) for part in thirds(dt * rate))
     mid = cum[rows - 1 : rows, :] * 0.5
     e_hi, e_lo = halves(jnp.exp(cum - mid))
     f_hi, f_lo = halves(jnp.exp(mid - cum) * dt)
@@ -236,6 +254,7 @@
     eh[:, LANES:] = e_lo
     fh[:, :LANES] = f_hi
     fh[:, LANES:] = f_lo
+    decay[...] = jnp.broadcast_to(jnp.exp(2.0 * mid), decay.shape)
     a_hi, a_lo = halves(jnp.broadcast_to(jnp.exp(mid), (16, LANES)))
     a_both = jnp.concatenate([a_hi, a_lo], axis=1)
 
@@ -299,41 +318,119 @@
             dcs[:, span] += mm(cot.astype(BF16), bs[:, span])
             dbs[:, span] += mm(cot.T.astype(BF16), cs[:, span])
 
-    def outer(q):
-        at = lax.div(q, per_group)
+    def wide(ref, q):
+        return jnp.concatenate([ref[q * sub + k] for k in range(sub)], axis=1)
+
+    def state_part(q, v, spread):
         here = lanes_of(q)
-        span = pl.ds(pl.multiple_of(at * STATE, STATE), STATE)
+        span = pl.ds(pl.multiple_of(lax.div(q, per_group) * STATE, STATE), STATE)
+        row[...] += fold(full(eg, eg_low, here) * mm(cs[:, span], v), spread)
+        dcs[:, span] += mm_nt(eg[:, here], v)
+
+    def cotangent_part(q, v, spread):
+        here = lanes_of(q)
+        span = pl.ds(pl.multiple_of(lax.div(q, per_group) * STATE, STATE), STATE)
+        col[...] += fold(full(fx, fx_low, here) * mm(bs[:, span], v), spread)
+        dbs[:, span] += mm_nt(fx[:, here], v)
+
+    def outer_near(q):
+        by = wide(scale, q)[0:1, :]
         spread = spread_of(q)
-        s_q = jnp.concatenate([s_in[q * sub + k] for k in range(sub)], axis=1)
-        t_q = jnp.concatenate([t_in[q * sub + k] for k in range(sub)], axis=1)
-        f_q = jnp.concatenate([fresh[q * sub + k] for k in range(sub)], axis=1)
-        row[...] += fold(full(eg, eg_low, here) * mm(cs[:, span], s_q), spread)
-        col[...] += fold(full(fx, fx_low, here) * mm(bs[:, span], t_q), spread)
-        dcs[:, span] += mm_nt(eg[:, here], s_q)
-        dbs[:, span] += mm_nt(fx[:, here], t_q)
-        whole = (s_q.astype(F32) + f_q) * t_q.astype(F32)
-        d_tail[...] += fold_line(jnp.sum(whole, axis=0, keepdims=True), spread)
+
+        @pl.when(side == 0)
+        def _():
+            v = (by * unpack(wide(recv_f, q))).astype(BF16)
+            kept[q] = v
+            state_part(q, v, spread)
+
+        @pl.when(side == 1)
+        def _():
+            v = (by * unpack(wide(recv_b, q))).astype(BF16)
+            kept[q] = v
+            cotangent_part(q, v, spread)
+
+    def outer_far(q):
+        by = wide(scale, q)[0:1, :]
+        spread = spread_of(q)
+        both = jnp.concatenate([spread, spread], axis=0)
+        past = jnp.concatenate(halves(jnp.broadcast_to(past_r[0:1, :], (16, LANES))), axis=1)
+        handed = mm(past, both)[0:1, :] * unpack(wide(recv_e, q))
+        f_q = wide(fresh, q)
+
+        def tail(s_q, t_q):
+            whole = (s_q.astype(F32) + f_q) * t_q.astype(F32)
+            d_tail[...] += fold_line(jnp.sum(whole, axis=0, keepdims=True), spread)
+
+        @pl.when(side == 1)
+        def _():
+            v = (by * (unpack(wide(recv_f, q)) + handed)).astype(BF16)
+            tail(v, kept[q])
+            state_part(q, v, spread)
+
+        @pl.when(side == 0)
+        def _():
+            v = (by * (unpack(wide(recv_b, q)) + handed)).astype(BF16)
+            tail(kept[q], v)
+            cotangent_part(q, v, spread)
+
+    def copy_to(src, dst, send_sem, recv_sem, other):
+        return pltpu.make_async_remote_copy(
+            src_ref=src, dst_ref=dst, send_sem=send_sem, recv_sem=recv_sem,
+            device_id={"ctx": other}, device_id_type=MESH,
+        )
 
     def up(k):
-        return pltpu.make_async_remote_copy(
-            src_ref=send_f.at[k], dst_ref=recv_f.at[k], send_sem=fs_sem.at[k], recv_sem=fr_sem.at[k],
-            device_id={"ctx": after}, device_id_type=MESH,
-        )
+        return copy_to(send_f.at[k], recv_f.at[k], fs_sem.at[k], fr_sem.at[k], chip_at(side, loc + 1))
 
     def down(k):
-        return pltpu.make_async_remote_copy(
-            src_ref=send_b.at[k], dst_ref=recv_b.at[k], send_sem=bs_sem.at[k], recv_sem=br_sem.at[k],
-            device_id={"ctx": before}, device_id_type=MESH,
-        )
-
-    far = (chips - 1) * SKEW
-    near = jnp.minimum(pos, chips - 1 - pos)
-    inner_from = jnp.where(near >= chips // 4, 2, near * SKEW + pieces)
-    inner_from = jnp.minimum(inner_from, far + sub - 1)
+        return copy_to(send_b.at[k], recv_b.at[k], bs_sem.at[k], br_sem.at[k], chip_at(side, loc - 1))
+
+    def over_f(k):
+        return copy_to(send_f.at[k], recv_e.at[k], fs_sem.at[k], er_sem.at[k], chip_at(1 - side, loc))
+
+    def over_b(k):
+        return copy_to(send_b.at[k], recv_e.at[k], bs_sem.at[k], er_sem.at[k], chip_at(1 - side, loc))
+
+    mid_len = run_len // 2
+    last = depth == run_len - 1
+    next_a = jnp.where(last, 0, jnp.where(depth < mid_len, depth + 1, depth - 1))
+    has_a = ((depth < mid_len - 1) | ((depth > mid_len) & (depth < run_len - 1))) | (
+        last & (run_len >= 2)
+    )
+    has_b = last & (run_len - 2 >= mid_len)
+
+    def on_a(k):
+        return copy_to(recv_e.at[k], recv_e.at[k], ea_sem.at[k], er_sem.at[k], at_depth(next_a))
+
+    def on_b(k):
+        return copy_to(
+            recv_e.at[k], recv_e.at[k], eb_sem.at[k], er_sem.at[k], at_depth(run_len - 2)
+        )
+
+    def past_on():
+        return copy_to(past_s, past_r, past_sem.at[0], past_sem.at[1], at_depth(depth + 1))
+
+    up_next = loc < run_len - 1
+    up_over = (loc == run_len - 1) & (side == 0)
+    down_next = loc > 0
+    down_over = (loc == 0) & (side == 1)
+    from_f = 1 + loc * SKEW + jnp.where(side == 1, DELAY, 0)
+    from_b = 1 + (run_len - 1 - loc) * SKEW + jnp.where(side == 0, DELAY, 0)
+    hops = jnp.where(last, 0, jnp.where(depth < mid_len, depth + 1, run_len - 1 - depth))
+    handed_at = 3 + run_len * SKEW
+    from_e = handed_at + hops * SKEW
+    far = handed_at + mid_len * SKEW
+    far_from = far + sub + 2
+    near_from = jnp.minimum(jnp.where(side == 0, from_f, from_b) + pieces + 1, far_from)
+    early = depth <= mid_len
+    gap = jnp.where(early, sub, 2)
+    inner_from = jnp.where(early, 2, (run_len - 1 - depth) * SKEW + pieces + 2)
+    inner_from = jnp.minimum(inner_from, far + sub + pieces - steps * gap - 1)
 
     def slot(t, carry):
-        k_f = t - pos * SKEW
-        k_b = t - (chips - 1 - pos) * SKEW
+        k_f = t - from_f
+        k_b = t - from_b
+        k_e = t - from_e
 
         @pl.when((t < sub * steps) & (lax.rem(t, sub) == 0))
         def _():
@@ -341,56 +438,94 @@
 
         @pl.when((k_f >= 0) & (k_f < pieces))
         def _():
-            @pl.when(pos > 0)
+            @pl.when(loc > 0)
             def _():
                 up(k_f).wait_recv()
 
-            by = scale[k_f][0:1, :]
-            entering = by * unpack(recv_f[k_f])
-            s_in[k_f] = entering.astype(BF16)
-
-            @pl.when(pos < chips - 1)
-            def _():
-                send_f[k_f] = pack(by * (entering + fresh[k_f]))
+            @pl.when(up_next | up_over)
+            def _():
+                by = scale[k_f][0:1, :]
+                send_f[k_f] = pack(by * (by * unpack(recv_f[k_f]) + fresh[k_f]))
+
+            @pl.when(up_next)
+            def _():
                 up(k_f).start()
 
+            @pl.when(up_over)
+            def _():
+                over_f(k_f).start()
+
         @pl.when((k_b >= 0) & (k_b < pieces))
         def _():
-            @pl.when(pos < chips - 1)
+            @pl.when(loc < run_len - 1)
             def _():
                 down(k_b).wait_recv()
 
-            by = scale[k_b][0:1, :]
-            entering = by * unpack(recv_b[k_b])
-            t_in[k_b] = entering.astype(BF16)
-
-            @pl.when(pos > 0)
-            def _():
-                send_b[k_b] = pack(by * (entering + back[k_b]))
+            @pl.when(down_next | down_over)
+            def _():
+                by = scale[k_b][0:1, :]
+                send_b[k_b] = pack(by * (by * unpack(recv_b[k_b]) + back[k_b]))
+
+            @pl.when(down_next)
+            def _():
                 down(k_b).start()
 
+            @pl.when(down_over)
+            def _():
+                over_b(k_b).start()
+
+        @pl.when((k_e >= 0) & (k_e < pieces))
+        def _():
+            on_a(k_e).wait_recv()
+
+            @pl.when(has_a)
+            def _():
+                on_a(k_e).start()
+
+            @pl.when(has_b)
+            def _():
+                on_b(k_e).start()
+
+        @pl.when(t == depth * SKEW + DELAY)
+        def _():
+            @pl.when(depth > 0)
+            def _():
+                past_on().wait_recv()
+
+            @pl.when(depth < run_len - 1)
+            def _():
+                past_s[...] = past_r[...] * decay[...]
+                past_on().start()
+
         k_i = t - inner_from
 
-        @pl.when((k_i >= 0) & (k_i < sub * steps) & (lax.rem(k_i, sub) == 0))
-        def _():
-            inner(lax.div(k_i, sub))
-
-        @pl.when(k_i == sub * steps)
+        @pl.when((k_i >= 0) & (k_i < steps * gap) & (lax.rem(k_i, gap) == 0))
+        def _():
+            inner(lax.div(k_i, gap))
+
+        @pl.when(k_i == steps * gap)
         def _():
             cross()
 
-        k_o = t - far - sub
-
-        @pl.when((k_o >= 0) & (lax.rem(k_o, sub) == 0))
-        def _():
-            outer(lax.div(k_o, sub))
-
-        return carry
-
-    lax.fori_loop(0, far + sub + pieces, slot, 0)
+        k_n = t - near_from
+
+        @pl.when((k_n >= 0) & (k_n < steps * sub) & (lax.rem(k_n, sub) == 0))
+        def _():
+            outer_near(lax.div(k_n, sub))
+
+        k_o = t - far_from
+
+        @pl.when((k_o >= 0) & (k_o < steps * sub) & (lax.rem(k_o, sub) == 0))
+        def _():
+            outer_far(lax.div(k_o, sub))
+
+        return carry
+
+    lax.fori_loop(0, far_from + pieces, slot, 0)
 
     z, dt, rate = step_sizes()
-    d_a = d_tail[0:1, :] + mm_exact((i_at <= j_at).astype(F32), row[...] - col[...])
+    ones = (i_at <= j_at).astype(F32).astype(BF16)
+    d_a = d_tail[0:1, :] + sum(mm(ones, part) for part in thirds(row[...] - col[...]))
     d_dt = col[...] / dt + rate * d_a
     d_raw = d_dt * jax.nn.sigmoid(z)
     sum_s[...] = jnp.zeros_like(sum_s)
@@ -427,8 +562,10 @@
         )
         copy.start()
         copies.append(copy)
-    gb[:, mine_b] = dbs[mine_rows, :]
-    gc[:, mine_b] = dcs[mine_rows, :]
+    own_b = pltpu.make_async_copy(dbs.at[mine_rows], gb.at[:, mine_b], own_sem.at[0])
+    own_c = pltpu.make_async_copy(dcs.at[mine_rows], gc.at[:, mine_b], own_sem.at[1])
+    own_b.start()
+    own_c.start()
 
     @pl.when(my_half == core)
     def _():
@@ -462,13 +599,21 @@
     lax.fori_loop(1, copies_dp, all_send, 0)
 
     def drain(k, carry):
-        @pl.when(pos < chips - 1)
+        @pl.when(up_next | up_over)
         def _():
             up(k).wait_send()
 
-        @pl.when(pos > 0)
+        @pl.when(down_next | down_over)
         def _():
             down(k).wait_send()
+
+        @pl.when(has_a)
+        def _():
+            on_a(k).wait_send()
+
+        @pl.when(has_b)
+        def _():
+            on_b(k).wait_send()
 
         return carry
 
@@ -486,16 +631,26 @@
         return carry
 
     lax.fori_loop(0, chips, drain_small, 0)
+
+    @pl.when(depth < run_len - 1)
+    def _():
+        past_on().wait_send()
+
     for copy in copies:
         copy.wait()
-    gs[...] = (draw_s[mine_rows, :] + draw_r[...]).astype(BF16)
+    gs_v[...] = (draw_s[mine_rows, :] + draw_r[...]).astype(BF16)
+    own_s = pltpu.make_async_copy(gs_v, gs, own_sem.at[2])
+    own_s.start()
     lax.fori_loop(1, copies_dp, all_wait, 0)
     all_r[0] = total
+    own_b.wait()
+    own_c.wait()
+    own_s.wait()
     heads = total.shape[1]
     head = lax.broadcasted_iota(jnp.int32, (heads, heads), 0)
     lane = lax.broadcasted_iota(jnp.int32, (heads, heads), 1)
-    pick = ((head == me * held + lane) & (lane < held)).astype(F32)
-    gp[...] = mm_exact(jnp.sum(all_r[...], axis=0), pick)
+    pick = ((head == me * held + lane) & (lane < held)).astype(F32).astype(BF16)
+    gp[...] = sum(mm(part, pick) for part in thirds(jnp.sum(all_r[...], axis=0)))
 
 
 def finish(gb, gc, gs, gp, gb_out, gc_out, gs_out, decay_out, bias_out, skip_out):
@@ -535,15 +690,17 @@
             jax.ShapeDtypeStruct((8, heads), F32),
         ),
         in_specs=[anywhere] * 5 + [scalars] * 2,
-        out_specs=(inside,) * 4,
+        out_specs=(anywhere,) * 3 + (inside,),
         scratch_shapes=[
             wide16, wide16,
             pltpu.VMEM((rows, cols), BF16), pltpu.VMEM((rows, cols), BF16),
             pltpu.VMEM((rows, heads), BF16),
             pltpu.VMEM((rows, 2 * LANES), BF16), pltpu.VMEM((rows, 2 * LANES), BF16),
             wide16, wide16, wide16, wide16,
-            state32, state32, state16, state16, state16, state16, state16, state16,
+            state32, state32, state16, state16, state16, state16, state16,
+            pltpu.VMEM((steps, STATE, WIDE), BF16),
             pltpu.VMEM((pieces, 8, LANES), F32),
+            tile, tile, tile,
             pltpu.VMEM((groups, rows, rows), F32),
             pltpu.VMEM((groups, rows, rows), BF16), pltpu.VMEM((groups, rows, rows), BF16),
             pltpu.VMEM((groups, STATE, rows), BF16), pltpu.VMEM((groups, STATE, rows), BF16),
@@ -551,11 +708,14 @@
             pltpu.VMEM((rows, cols), F32), pltpu.VMEM((rows, cols), F32),
             tile, tile,
             pltpu.VMEM((rows, heads), F32), pltpu.VMEM((tok, heads), F32),
+            pltpu.VMEM((tok, heads), BF16),
             tile, pltpu.VMEM((chips, 8, heads), F32),
             tile, pltpu.VMEM((chips, 8, heads), F32),
             tile, pltpu.VMEM((copies_dp, 8, heads), F32),
             dma((moves,)), dma((moves,)), dma((moves,)),
             dma((pieces,)), dma((pieces,)), dma((pieces,)), dma((pieces,)),
+            dma((pieces,)), dma((pieces,)), dma((pieces,)),
+            dma((2,)),
             dma((3,)), dma((3,)),
             dma((chips,)), dma((chips,)), dma((chips,)), dma((chips,)),
             dma((copies_dp,)), dma((copies_dp,)),

time: 116 us -> 111 us (0.957)
  Pallas kernels: 115 us -> 110 us
    pallas_call x1, Pallas kernels: 113 us -> 108 us  [run(): pl.pallas_call(partial(kernel, chips, copies_dp), out_shape=(jax.ShapeDty...]
where the time goes in v3:
time: 111 us
  Pallas kernels  110 us (99%)
    pallas_call x1, Pallas kernels, run(): pl.pallas_call(partial(kernel, chips, copies_dp), out_shape=(jax.ShapeDty...  108 us

profile of v3, /device:TPU:1, one launch (start us, length us, event | category | flops | bytes accessed | tf_op | source)
XLA Modules:
  0.0 110.9 jit_solution(4370741252434985585)
XLA Ops:
  0.6 108.4 %scan_backward.1 = (f32[128,512]{1,0:T(8,128)}, f32[128,512]{1,0:T(8,128)}, bf16[128,128]{1,0:T(8,128)(2,1)}, f32[8,128]{1,0:T(8,128)}) custom-call(bf16[128,8192]{1,0:T(8,128)(2,1)} %bitcast.11, bf16[128,8192]{1,0:T(8,128)(2,1)} %bitcast.12, bf16[128,512]{1,0:T(8,128)(2,1)} %bitcast.13, bf16[128,512]{1,0:T(8,128)(2,1)} %bitcast.14, ...), custom_call_target="tpu_custom_call" | custom-call | tf_op jit(solution)/shard_map/scan_backward/pallas_call | solution.py:684
  109.0 1.9 %results.1 = (f32[128,512]{1,0:T(8,128)}, f32[128,512]{1,0:T(8,128)}, bf16[128,128]{1,0:T(8,128)(2,1)}, f32[1,4]{1,0:T(1,128)}, f32[1,4]{1,0:T(1,128)}, /*index=5*/f32[1,4]{1,0:T(1,128)}) custom-call(f32[128,512]{1,0:T(8,128)} %get-tuple-element.16.gb, f32[128,512]{1,0:T(8,128)} %get-tuple-element.17.gc, bf16[128,128]{1,0:T(8,128)(2,1)} %get-tuple-element.18.gs, ...), custom_call_target="tpu_custom_call" | custom-call | tf_op jit(solution)/shard_map/results/pallas_call | solution.py:729

commit v4 on v3

--- a/solution.py
+++ b/solution.py
@@ -324,13 +324,13 @@
     def state_part(q, v, spread):
         here = lanes_of(q)
         span = pl.ds(pl.multiple_of(lax.div(q, per_group) * STATE, STATE), STATE)
-        row[...] += fold(full(eg, eg_low, here) * mm(cs[:, span], v), spread)
+        row[...] += mm_nt((full(eg, eg_low, here) * mm(cs[:, span], v)).astype(BF16), spread)
         dcs[:, span] += mm_nt(eg[:, here], v)
 
     def cotangent_part(q, v, spread):
         here = lanes_of(q)
         span = pl.ds(pl.multiple_of(lax.div(q, per_group) * STATE, STATE), STATE)
-        col[...] += fold(full(fx, fx_low, here) * mm(bs[:, span], v), spread)
+        col[...] += mm_nt((full(fx, fx_low, here) * mm(bs[:, span], v)).astype(BF16), spread)
         dbs[:, span] += mm_nt(fx[:, here], v)
 
     def outer_near(q):
@@ -422,7 +422,7 @@
     far = handed_at + mid_len * SKEW
     far_from = far + sub + 2
     near_from = jnp.minimum(jnp.where(side == 0, from_f, from_b) + pieces + 1, far_from)
-    early = depth <= mid_len
+    early = depth <= run_len
     gap = jnp.where(early, sub, 2)
     inner_from = jnp.where(early, 2, (run_len - 1 - depth) * SKEW + pieces + 2)
     inner_from = jnp.minimum(inner_from, far + sub + pieces - steps * gap - 1)

time: 111 us -> 110 us (level)
    pallas_call x1, Pallas kernels: 108 us -> 107 us  [run(): pl.pallas_call(partial(kernel, chips, copies_dp), out_shape=(jax.ShapeDty...]
where the time goes in v4:
time: 110 us; the launch traced here: 109 us
  Pallas kernels  109 us (99%)
    pallas_call x1, Pallas kernels, run(): pl.pallas_call(partial(kernel, chips, copies_dp), out_shape=(jax.ShapeDty...  107 us

profile of v4, /device:TPU:1, one launch (start us, length us, event | category | flops | bytes accessed | tf_op | source)
XLA Modules:
  0.0 109.4 jit_solution(3727556386687257267)
XLA Ops:
  0.6 106.9 %scan_backward.1 = (f32[128,512]{1,0:T(8,128)}, f32[128,512]{1,0:T(8,128)}, bf16[128,128]{1,0:T(8,128)(2,1)}, f32[8,128]{1,0:T(8,128)}) custom-call(bf16[128,8192]{1,0:T(8,128)(2,1)} %bitcast.11, bf16[128,8192]{1,0:T(8,128)(2,1)} %bitcast.12, bf16[128,512]{1,0:T(8,128)(2,1)} %bitcast.13, bf16[128,512]{1,0:T(8,128)(2,1)} %bitcast.14, ...), custom_call_target="tpu_custom_call" | custom-call | tf_op jit(solution)/shard_map/scan_backward/pallas_call | solution.py:684
  107.5 1.9 %results.1 = (f32[128,512]{1,0:T(8,128)}, f32[128,512]{1,0:T(8,128)}, bf16[128,128]{1,0:T(8,128)(2,1)}, f32[1,4]{1,0:T(1,128)}, f32[1,4]{1,0:T(1,128)}, /*index=5*/f32[1,4]{1,0:T(1,128)}) custom-call(f32[128,512]{1,0:T(8,128)} %get-tuple-element.16.gb, f32[128,512]{1,0:T(8,128)} %get-tuple-element.17.gc, bf16[128,128]{1,0:T(8,128)(2,1)} %get-tuple-element.18.gs, ...), custom_call_target="tpu_custom_call" | custom-call | tf_op jit(solution)/shard_map/results/pallas_call | solution.py:729
